TPU v7x, 32 devices: a whole 2x2x4 slice. The times are simulated.
32 devices in a mesh: groups: 2 (over x), col: 8 (over z, y), row: 2 (over core).
Axes of the slice: x: 2, y: 2, z: 4, core: 2. Of those that a mesh axis runs over, the one named last changes fastest.
Arguments:
- points: bfloat16 [64, 3072], P(None, ('groups', 'col', 'row')), parts along dimension 1, may hold values from -6 to 6
- sketch: float32 [3072, 256], P(('groups', 'col', 'row')), parts along dimension 0, may hold values from -6 to 6
Outputs:
- basis: float32 [3072, 256], P(('groups', 'col', 'row')), parts along dimension 0
- factor: float32 [512, 256], P('groups'), parts along dimension 0
There are 2 independent parts, one for each index of `groups`. A program takes and returns all parts, laid end to end along the dimension named above; each array names one. Nothing has to cross between parts.
All inputs are finite; a program needn't handle non-finite values.
Results may differ from a plain program's by a relative error of at most 0.0003.
Values may be sent and summed in bfloat16 or wider, within the bound.
A program may use at most 64 MiB of HBM per device.

v0:
```python
import jax
import jax.numpy as jnp
from jax import lax
from jax.sharding import PartitionSpec as P

PASSES = 2


def kernel_rows(block_t, cols_t, gamma):
    block_f = block_t.astype(jnp.float32)
    cols_f = cols_t.astype(jnp.float32)
    block_sq = jnp.sum(block_f * block_f, axis=0)
    cols_sq = jnp.sum(cols_f * cols_f, axis=0)
    cross = lax.dot_general(
        block_t, cols_t, (((0,), (0,)), ((), ())), preferred_element_type=jnp.float32
    )
    return jnp.exp(-gamma * (block_sq[:, None] + cols_sq[None, :] - 2.0 * cross))


def orthonormal(ymat, block_count):
    local_gram = jnp.dot(ymat.T, ymat, precision=lax.Precision.HIGHEST)
    gram = lax.psum(local_gram, ("col", "row")) / block_count
    lower = jnp.linalg.cholesky(gram)
    qmat = jax.scipy.linalg.solve_triangular(lower, ymat.T, lower=True).T
    return (qmat, lower.T)


def local(points, sketch):
    feats, own = points.shape
    block_count = own * lax.axis_size("col") * lax.axis_size("row")
    gamma = ((block_count / 32.0) ** (2.0 / feats) - 1.0) / 4.0
    row_pts = lax.all_gather(points, "row", axis=1, tiled=True)
    col_pts = lax.all_gather(points, "col", axis=1, tiled=True)

    def tile_at():
        return kernel_rows(row_pts, col_pts, gamma)

    def accumulate_fragment(piece):
        kernel_tile = tile_at()
        return jnp.dot(
            kernel_tile, piece, precision=lax.Precision.HIGHEST, preferred_element_type=jnp.float32
        )

    def apply_operator(vector_matrix):
        running_sum = accumulate_fragment(lax.all_gather(vector_matrix, "col", axis=0, tiled=True))
        return lax.psum_scatter(running_sum, "row", scatter_dimension=0, tiled=True)

    ymat = apply_operator(sketch)
    for step in range(PASSES):
        qmat, upper = orthonormal(ymat, block_count)
        ymat = apply_operator(qmat)
    basis, factor = orthonormal(ymat, block_count)
    return (basis, factor)


def solution(mesh):
    in_specs = (P(None, ("groups", "col", "row")), P(("groups", "col", "row"), None))
    out_specs = (P(("groups", "col", "row"), None), P("groups", None))
    return jax.shard_map(local, mesh=mesh, in_specs=in_specs, out_specs=out_specs, check_vma=False)
```

profile of v0, /device:TPU:0, one launch (start us, length us, event | category | flops | bytes accessed | tf_op | source)
XLA Modules:
  0.0 657.9 jit_solution(15062944571670250441)
XLA Ops:
  7.2 32.5 %all-gather.1 = bf16[8,96,64]{1,2,0:T(8,128)(2,1)S(1)} all-gather(bf16[1,96,64]{1,2,0:T(8,128)(2,1)} %bitcast.131), channel_id=1, replica_groups=mesh['groups'=2,'col'=8,'row'=2] {'col'}, dimensions={0}, use_global_device_ids=true | all-gather | bytes 110592 | tf_op jit(solution)/shard_map/all_gather | solution.py:33
  39.7 1.8 all-gather
  42.7 32.2 %all_gather.17 = f32[768,256]{1,0:T(8,128)S(1)} all-gather(f32[96,256]{1,0:T(8,128)S(1)} %copy-done.6), channel_id=1, replica_groups=mesh['groups'=2,'col'=8,'row'=2] {'col'}, dimensions={0}, use_global_device_ids=true | all-gather | bytes 884736 | tf_op jit(solution)/shard_map/all_gather | solution.py:45
  76.7 8.6 %reduce-scatter.4.cloned.1.call-done = f32[96,256]{1,0:T(8,128)} async-done(((f32[192,256]{1,0:T(8,128)}), f32[96,256]{1,0:T(8,128)}) %reduce-scatter.4.cloned.1.call-update) | async-done | bytes 98320 | tf_op jit(solution)/shard_map/reduce_scatter | solution.py:46
  85.3 2.1 fusion.42
  87.5 91.7 %all-reduce.5.cloned.1.call-done = f32[256,256]{0,1:T(8,128)} async-done(((f32[256,256]{0,1:T(8,128)}), f32[256,256]{0,1:T(8,128)}) %all-reduce.5.cloned.1.call-update) | async-done | bytes 262160 | tf_op jit(solution)/shard_map/psum | solution.py:22
  181.2 11.7 %cholesky.172 = f32[128,128]{1,0:T(8,128)S(1)} custom-call(f32[128,128]{1,0:T(8,128)S(1)} %cholesky.270), custom_call_target="Cholesky" | custom-call | tf_op jit(solution)/shard_map/jit(cholesky)/cholesky | solution.py:23
  192.9 9.8 %custom-call.15 = f32[1,128,128]{1,2,0:T(8,128)S(1)} custom-call(f32[1,128,128]{2,1,0:T(8,128)S(1)} %get-tuple-element.76), custom_call_target="InvertDiagBlocksLowerTriangular" | custom-call | tf_op jit(solution)/shard_map/jit(cholesky)/cholesky | solution.py:23
  203.3 11.7 %cholesky.189 = f32[128,128]{1,0:T(8,128)S(1)} custom-call(f32[128,128]{1,0:T(8,128)S(1)} %convolution_subtract_fusion.2), custom_call_target="Cholesky" | custom-call | tf_op jit(solution)/shard_map/jit(cholesky)/cholesky | solution.py:23
  217.2 4.4 while.6
  218.1 1.4 bitcast_dynamic-update-slice_fusion.6
  221.6 19.7 %custom-call.16 = f32[2,128,128]{1,2,0:T(8,128)S(1)} custom-call(f32[2,128,128]{2,1,0:T(8,128)S(1)} %get-tuple-element.24), custom_call_target="InvertDiagBlocksLowerTriangular" | custom-call | tf_op jit(solution)/shard_map/jit(_solve_triangular)/triangular_solve | solution.py:24
  242.0 32.9 %all_gather.18 = f32[768,256]{1,0:T(8,128)S(1)} all-gather(f32[96,256]{1,0:T(8,128)S(1)} %maximum_bitcast_fusion), channel_id=1, replica_groups=mesh['groups'=2,'col'=8,'row'=2] {'col'}, dimensions={0}, use_global_device_ids=true | all-gather | bytes 884736 | tf_op jit(solution)/shard_map/all_gather | solution.py:45
  276.3 7.3 %reduce-scatter.6.cloned.1.call-done = f32[96,256]{1,0:T(8,128)} async-done(((f32[192,256]{1,0:T(8,128)}), f32[96,256]{1,0:T(8,128)}) %reduce-scatter.6.cloned.1.call-update) | async-done | bytes 98320 | tf_op jit(solution)/shard_map/reduce_scatter | solution.py:46
  283.6 2.1 fusion.44
  285.8 91.7 %all-reduce.7.cloned.1.call-done = f32[256,256]{0,1:T(8,128)} async-done(((f32[256,256]{0,1:T(8,128)}), f32[256,256]{0,1:T(8,128)}) %all-reduce.7.cloned.1.call-update) | async-done | bytes 262160 | tf_op jit(solution)/shard_map/psum | solution.py:22
  379.4 11.7 %cholesky.206 = f32[128,128]{1,0:T(8,128)S(1)} custom-call(f32[128,128]{1,0:T(8,128)S(1)} %cholesky.273), custom_call_target="Cholesky" | custom-call | tf_op jit(solution)/shard_map/jit(cholesky)/cholesky | solution.py:23
  391.2 9.8 %custom-call.17 = f32[1,128,128]{1,2,0:T(8,128)S(1)} custom-call(f32[1,128,128]{2,1,0:T(8,128)S(1)} %get-tuple-element.72), custom_call_target="InvertDiagBlocksLowerTriangular" | custom-call | tf_op jit(solution)/shard_map/jit(cholesky)/cholesky | solution.py:23
  401.5 11.7 %cholesky.223 = f32[128,128]{1,0:T(8,128)S(1)} custom-call(f32[128,128]{1,0:T(8,128)S(1)} %convolution_subtract_fusion.1), custom_call_target="Cholesky" | custom-call | tf_op jit(solution)/shard_map/jit(cholesky)/cholesky | solution.py:23
  416.0 14.2 %while.7 = (s32[]{:T(128)}, f32[256,256]{1,0:T(8,128)S(1)}, s32[2,2]{1,0:T(2,128)S(1)}, f32[2,128,128]{2,1,0:T(8,128)S(1)}, s32[]{:T(128)}) while((s32[]{:T(128)}, f32[256,256]{1,0:T(8,128)S(1)}, s32[2,2]{1,0:T(2,128)S(1)}, f32[2,128,128]{2,1,0:T(8,128)S(1)}, s32[]{:T(128)}) %tuple.89), condition=%wide.while_cond.clone, body=%wide.while_body.clone.sunk | while | flops 2 | bytes 131181 | solution.py:24
  426.8 1.4 bitcast_dynamic-update-slice_fusion.7
  428.8 1.4 bitcast_dynamic-update-slice_fusion.7
  430.3 19.7 %custom-call.18 = f32[2,128,128]{1,2,0:T(8,128)S(1)} custom-call(f32[2,128,128]{2,1,0:T(8,128)S(1)} %get-tuple-element.25), custom_call_target="InvertDiagBlocksLowerTriangular" | custom-call | tf_op jit(solution)/shard_map/jit(_solve_triangular)/triangular_solve | solution.py:24
  450.6 32.9 %all_gather.19 = f32[768,256]{1,0:T(8,128)S(1)} all-gather(f32[96,256]{1,0:T(8,128)S(1)} %maximum_bitcast_fusion.1), channel_id=1, replica_groups=mesh['groups'=2,'col'=8,'row'=2] {'col'}, dimensions={0}, use_global_device_ids=true | all-gather | bytes 884736 | tf_op jit(solution)/shard_map/all_gather | solution.py:45
  484.9 7.3 %reduce-scatter.8.cloned.1.call-done = f32[96,256]{1,0:T(8,128)} async-done(((f32[192,256]{1,0:T(8,128)}), f32[96,256]{1,0:T(8,128)}) %reduce-scatter.8.cloned.1.call-update) | async-done | bytes 98320 | tf_op jit(solution)/shard_map/reduce_scatter | solution.py:46
  492.3 2.1 fusion.46
  494.4 91.7 %all-reduce.9.cloned.1.call-done = f32[256,256]{0,1:T(8,128)} async-done(((f32[256,256]{0,1:T(8,128)}), f32[256,256]{0,1:T(8,128)}) %all-reduce.9.cloned.1.call-update) | async-done | bytes 262160 | tf_op jit(solution)/shard_map/psum | solution.py:22
  588.1 11.7 %cholesky.240 = f32[128,128]{1,0:T(8,128)S(1)} custom-call(f32[128,128]{1,0:T(8,128)S(1)} %cholesky.276), custom_call_target="Cholesky" | custom-call | tf_op jit(solution)/shard_map/jit(cholesky)/cholesky | solution.py:23
  599.9 9.8 %custom-call.19 = f32[1,128,128]{1,2,0:T(8,128)S(1)} custom-call(f32[1,128,128]{2,1,0:T(8,128)S(1)} %get-tuple-element.68), custom_call_target="InvertDiagBlocksLowerTriangular" | custom-call | tf_op jit(solution)/shard_map/jit(cholesky)/cholesky | solution.py:23
  610.2 11.7 %cholesky.257 = f32[128,128]{1,0:T(8,128)S(1)} custom-call(f32[128,128]{1,0:T(8,128)S(1)} %convolution_subtract_fusion), custom_call_target="Cholesky" | custom-call | tf_op jit(solution)/shard_map/jit(cholesky)/cholesky | solution.py:23
  624.7 4.3 while.8
  629.0 19.7 %custom-call.20 = f32[2,128,128]{1,2,0:T(8,128)S(1)} custom-call(f32[2,128,128]{2,1,0:T(8,128)S(1)} %get-tuple-element.26), custom_call_target="InvertDiagBlocksLowerTriangular" | custom-call | tf_op jit(solution)/shard_map/jit(_solve_triangular)/triangular_solve | solution.py:24
  (106 shorter events, 28.4 us)
Async XLA Ops:
  7.2 78.1 %reduce-scatter.4.cloned.1.call-start = ((), (), s32[]{:S(2)}) async-start(), calls=%async_computation.3 | async-start | bytes 294912 | tf_op jit(solution)/shard_map/reduce_scatter | solution.py:46
  7.2 32.5 %copy-start.7 = (bf16[64,96]{1,0:T(8,128)(2,1)S(1)}, bf16[64,96]{1,0:T(8,128)(2,1)}, u32[]{:S(2)}) copy-start(bf16[64,96]{1,0:T(8,128)(2,1)} %param.5) | copy-start | bytes 36868
  41.8 0.9 copy-start.6
  76.6 102.6 %all-reduce.5.cloned.1.call-start = ((), (), s32[]{:S(2)}) async-start(), calls=%async_computation.4 | async-start | bytes 524288 | tf_op jit(solution)/shard_map/psum | solution.py:22
  87.4 196.2 %reduce-scatter.6.cloned.1.call-start = ((), (), s32[]{:S(2)}) async-start(), calls=%async_computation.5 | async-start | bytes 294912 | tf_op jit(solution)/shard_map/reduce_scatter | solution.py:46
  180.2 1.0 copy-start
  217.2 24.1 %copy-start.3 = (f32[96,256]{1,0:T(8,128)S(1)}, f32[96,256]{1,0:T(8,128)}, u32[]{:S(2)}) copy-start(f32[96,256]{1,0:T(8,128)} %reduce-scatter.4.cloned.1.call-done) | copy-start | bytes 294916
  276.2 101.2 %all-reduce.7.cloned.1.call-start = ((), (), s32[]{:S(2)}) async-start(), calls=%async_computation.6 | async-start | bytes 524288 | tf_op jit(solution)/shard_map/psum | solution.py:22
  285.7 206.5 %reduce-scatter.8.cloned.1.call-start = ((), (), s32[]{:S(2)}) async-start(), calls=%async_computation.7 | async-start | bytes 294912 | tf_op jit(solution)/shard_map/reduce_scatter | solution.py:46
  378.4 1.0 copy-start.1
  416.0 33.9 %copy-start.5 = (f32[96,256]{1,0:T(8,128)S(1)}, f32[96,256]{1,0:T(8,128)}, u32[]{:S(2)}) copy-start(f32[96,256]{1,0:T(8,128)} %reduce-scatter.6.cloned.1.call-done) | copy-start | bytes 294916
  484.9 101.2 %all-reduce.9.cloned.1.call-start = ((), (), s32[]{:S(2)}) async-start(), calls=%async_computation.8 | async-start | bytes 524288 | tf_op jit(solution)/shard_map/psum | solution.py:22
  587.1 1.0 copy-start.2
  624.7 24.0 %copy-start.4 = (f32[96,256]{1,0:T(8,128)S(1)}, f32[96,256]{1,0:T(8,128)}, u32[]{:S(2)}) copy-start(f32[96,256]{1,0:T(8,128)} %reduce-scatter.8.cloned.1.call-done) | copy-start | bytes 294916
Sparse Core Ops, SparseCore 0:
  76.8 8.4 reduce-scatter.3
  89.3 89.9 all-reduce.4
  276.4 7.2 reduce-scatter.5
  287.4 89.9 all-reduce.6
  485.0 7.2 reduce-scatter.7
  496.1 89.9 all-reduce.8
where the time goes:
time: 663 us; the launch traced here: 658 us
  waiting for transfers between devices  299 us (45%)
  other arithmetic  166 us (25%)
  blocking collectives  132 us (20%)
  between operations  18.8 us (3%)
  local copies, waits for them, and re-layouts  17.1 us (3%)
  matrix products  14 us (2%)
  loops' own time  10.7 us (2%)
    psum x3, waiting for transfers between devices, orthonormal(): gram = lax.psum(local_gram, ('col', 'row')) / block_count  275 us
    another operation x20, other arithmetic, orthonormal(): lower = jnp.linalg.cholesky(gram)  103 us
    all_gather x3, blocking collectives, apply_operator(): lax.all_gather(vector_matrix, 'col', axis=0, tiled=True)  98 us
    another operation x6, other arithmetic, orthonormal(): qmat = jax.scipy.linalg.solve_triangular(lower, ymat.T, lower=True).T  59.1 us
    all_gather x1, blocking collectives, local(): col_pts = lax.all_gather(points, 'col', axis=1, tiled=True)  32.5 us
    reduce_scatter x3, waiting for transfers between devices, apply_operator(): return lax.psum_scatter(running_sum, 'row', scatter_dimension=0, tiled=True)  23.3 us
  transfers between devices with their start and end apart: 6, of which 6 were waited for; matrix products, arithmetic and copies ran while one was open for 0% of the time, Pallas kernels for 0%

commit v1 on v0

--- a/solution.py
+++ b/solution.py
@@ -1,9 +1,143 @@
+import functools
+
 import jax
 import jax.numpy as jnp
 from jax import lax
+from jax.experimental import pallas as pl
+from jax.experimental.pallas import tpu as pltpu
 from jax.sharding import PartitionSpec as P
 
 PASSES = 2
+HIGHEST = lax.Precision.HIGHEST
+MAX_POINTS = 2048
+ROWS = 256
+HALF = 128
+
+
+def dot(a, b, dims, precision=None):
+    return lax.dot_general(
+        a, b, (dims, ((), ())), precision=precision, preferred_element_type=jnp.float32
+    )
+
+
+def split(x):
+    high = x.astype(jnp.bfloat16)
+    low = (x - high.astype(jnp.float32)).astype(jnp.bfloat16)
+    return high, low
+
+
+def factor_block(block):
+    row = lax.broadcasted_iota(jnp.int32, (HALF, HALF), 0)
+    lane = lax.broadcasted_iota(jnp.int32, (HALF, HALF), 1)
+    sub = lax.broadcasted_iota(jnp.int32, (8, HALF), 0)
+    a = block
+    i = jnp.where(row == lane, 1.0, 0.0).astype(jnp.float32)
+    done_a, done_i = [], []
+    for k in range(0, HALF, 8):
+        cols = [jnp.broadcast_to(a[:, k + j : k + j + 1], a.shape) for j in range(8)]
+        head_a, head_i = a[:8], i[:8]
+        mults, rows_a, rows_i = [], [], []
+        for j in range(8):
+            r = lax.rsqrt(cols[j][j : j + 1])
+            m = cols[j] * r
+            for n in range(j + 1, 8):
+                cols[n] = cols[n] - m * (cols[n][j : j + 1] * r)
+            row_a, row_i = head_a[j : j + 1] * r, head_i[j : j + 1] * r
+            below = jnp.where(sub > j, m[:8], 0.0)
+            head_a = jnp.where(sub == j, row_a, head_a - below * row_a)
+            head_i = jnp.where(sub == j, row_i, head_i - below * row_i)
+            mults.append(m)
+            rows_a.append(row_a)
+            rows_i.append(row_i)
+        done_a.append(head_a)
+        done_i.append(head_i)
+        if k + 8 < HALF:
+            a, i = a[8:], i[8:]
+            for j in range(8):
+                a = a - mults[j][8:] * rows_a[j]
+                i = i - mults[j][8:] * rows_i[j]
+    upper = jnp.where(row <= lane, jnp.concatenate(done_a, axis=0), 0.0)
+    return upper, jnp.concatenate(done_i, axis=0)
+
+
+def part_kernel(gamma, pts, sketch, basis, factor, high, low, v, vh, vl, y, inv):
+    feats, count = pts.shape
+    own = basis.shape[0]
+    me = lax.axis_index("col") * lax.axis_size("row") + lax.axis_index("row")
+    all_f = pts[...].astype(jnp.float32)
+    all_sq = jnp.sum(all_f * all_f, axis=0, keepdims=True)
+    ones = jnp.ones((feats, HALF), jnp.float32)
+    for at in range(0, count, ROWS):
+        rows = pts[:, at : at + ROWS]
+        rows_f = rows.astype(jnp.float32)
+        rows_sq = dot(rows_f * rows_f, ones, ((0,), (0,)), HIGHEST)[:, :1]
+        cross = dot(rows, pts[...], ((0,), (0,)))
+        h, l = split(jnp.exp(-gamma * (rows_sq + all_sq - 2.0 * cross)))
+        high[at : at + ROWS] = h
+        low[at : at + ROWS] = l
+    v[...] = sketch[...]
+
+    def one_pass(step, carry):
+        h, l = split(v[...])
+        vh[...] = h
+        vl[...] = l
+
+        def apply_rows(b, c):
+            at = pl.ds(pl.multiple_of(b * ROWS, ROWS), ROWS)
+            kh, kl = high[at, :], low[at, :]
+            d = ((1,), (0,))
+            y[at, :] = dot(kh, vh[...], d) + (dot(kh, vl[...], d) + dot(kl, vh[...], d))
+            return c
+
+        lax.fori_loop(0, count // ROWS, apply_rows, 0)
+        ym = y[...]
+        gram = dot(ym, ym, ((0,), (0,)), HIGHEST) / count
+        u11, i11 = factor_block(gram[:HALF, :HALF])
+        u12 = dot(i11, gram[:HALF, HALF:], ((1,), (0,)), HIGHEST)
+        rest = gram[HALF:, HALF:] - dot(u12, u12, ((0,), (0,)), HIGHEST)
+        u22, i22 = factor_block(rest)
+        i21 = -dot(i22, dot(u12, i11, ((0,), (0,)), HIGHEST), ((1,), (0,)), HIGHEST)
+        factor[:HALF, :HALF] = u11
+        factor[:HALF, HALF:] = u12
+        factor[HALF:, :HALF] = jnp.zeros_like(u11)
+        factor[HALF:, HALF:] = u22
+        inv[:HALF, :HALF] = i11
+        inv[:HALF, HALF:] = jnp.zeros_like(i11)
+        inv[HALF:, :HALF] = i21
+        inv[HALF:, HALF:] = i22
+        v[...] = dot(ym, inv[...], ((1,), (1,)), HIGHEST)
+        return carry
+
+    lax.fori_loop(0, PASSES + 1, one_pass, 0)
+    basis[...] = v[pl.ds(pl.multiple_of(me * own, 8), own), :]
+
+
+def whole_part(points, sketch):
+    feats, own = points.shape
+    rank = sketch.shape[1]
+    count = own * lax.axis_size("col") * lax.axis_size("row")
+    gamma = ((count / 32.0) ** (2.0 / feats) - 1.0) / 4.0
+    pts = lax.all_gather(points, ("col", "row"), axis=1, tiled=True)
+    full = lax.all_gather(sketch, ("col", "row"), axis=0, tiled=True)
+    return pl.pallas_call(
+        functools.partial(part_kernel, gamma),
+        out_shape=(
+            jax.ShapeDtypeStruct((own, rank), jnp.float32),
+            jax.ShapeDtypeStruct((rank, rank), jnp.float32),
+        ),
+        in_specs=[pl.BlockSpec(memory_space=pltpu.VMEM)] * 2,
+        out_specs=[pl.BlockSpec(memory_space=pltpu.VMEM)] * 2,
+        scratch_shapes=[
+            pltpu.VMEM((count, count), jnp.bfloat16),
+            pltpu.VMEM((count, count), jnp.bfloat16),
+            pltpu.VMEM((count, rank), jnp.float32),
+            pltpu.VMEM((count, rank), jnp.bfloat16),
+            pltpu.VMEM((count, rank), jnp.bfloat16),
+            pltpu.VMEM((count, rank), jnp.float32),
+            pltpu.VMEM((rank, rank), jnp.float32),
+        ],
+        compiler_params=pltpu.CompilerParams(vmem_limit_bytes=50 * 1024 * 1024),
+    )(pts, full)
 
 
 def kernel_rows(block_t, cols_t, gamma):
@@ -25,7 +159,7 @@
     return (qmat, lower.T)
 
 
-def local(points, sketch):
+def split_part(points, sketch):
     feats, own = points.shape
     block_count = own * lax.axis_size("col") * lax.axis_size("row")
     gamma = ((block_count / 32.0) ** (2.0 / feats) - 1.0) / 4.0
@@ -53,6 +187,14 @@
     return (basis, factor)
 
 
+def local(points, sketch):
+    count = points.shape[1] * lax.axis_size("col") * lax.axis_size("row")
+    small = count <= MAX_POINTS and count % ROWS == 0
+    if small and sketch.shape[1] == 2 * HALF and points.shape[1] % 8 == 0:
+        return whole_part(points, sketch)
+    return split_part(points, sketch)
+
+
 def solution(mesh):
     in_specs = (P(None, ("groups", "col", "row")), P(("groups", "col", "row"), None))
     out_specs = (P(("groups", "col", "row"), None), P("groups", None))

time: 663 us -> 118 us (0.18)
  waiting for transfers between devices: 299 us -> 21.1 us
  other arithmetic: 166 us -> 0 us
  blocking collectives: 132 us -> 24.1 us
  Pallas kernels: 0 us -> 57.2 us
  local copies, waits for them, and re-layouts: 17.1 us -> 1.84 us
  matrix products: 14 us -> 0 us
  loops' own time: 10.7 us -> 0 us
    psum x3 -> x0, waiting for transfers between devices: 275 us -> none  [orthonormal(): gram = lax.psum(local_gram, ('col', 'row')) / block_count]
    another operation x26 -> x0, other arithmetic: 162 us -> none  [the longest x20 103 us: orthonormal(): lower = jnp.linalg.cholesky(gram)]
    all_gather x5 -> x1, blocking collectives: 132 us -> 24.1 us  [whole_part(): pts = lax.all_gather(points, ('col', 'row'), axis=1, tiled=True)]
    pallas_call x0 -> x1, Pallas kernels: none -> 57.2 us  [whole_part(): pl.pallas_call(functools.partial(part_kernel, gamma), out_shape=(jax.Shap...]
    reduce_scatter x3 -> x0, waiting for transfers between devices: 23.3 us -> none  [apply_operator(): return lax.psum_scatter(running_sum, 'row', scatter_dimension=0, tiled=True)]
    all_gather x0 -> x1, waiting for transfers between devices: none -> 20.5 us  [whole_part(): full = lax.all_gather(sketch, ('col', 'row'), axis=0, tiled=True)]
    another operation x28 -> x0, local copies, waits for them, and re-layouts: 12.3 us -> none  [the longest x22 12.3 us: orthonormal(): qmat = jax.scipy.linalg.solve_triangular(lower, ymat.T, lower=True).T]
    another operation x3 -> x0, loops' own time: 10.7 us -> none  [orthonormal(): qmat = jax.scipy.linalg.solve_triangular(lower, ymat.T, lower=True).T]
  transfers between devices with their start and end apart: 6 -> 1, of which waited for: 6 -> 1; matrix products, arithmetic and copies ran while one was open for 0% -> 0% of each run, Pallas kernels for 0% -> 0%
where the time goes in v1:
time: 118 us
  Pallas kernels  57.2 us (48%)
  blocking collectives  24.1 us (20%)
  waiting for transfers between devices  21.1 us (18%)
  between operations  14 us (12%)
  local copies, waits for them, and re-layouts  1.84 us (2%)
    pallas_call x1, Pallas kernels, whole_part(): pl.pallas_call(functools.partial(part_kernel, gamma), out_shape=(jax.Shap...  57.2 us
    all_gather x1, blocking collectives, whole_part(): pts = lax.all_gather(points, ('col', 'row'), axis=1, tiled=True)  24.1 us
    all_gather x1, waiting for transfers between devices, whole_part(): full = lax.all_gather(sketch, ('col', 'row'), axis=0, tiled=True)  20.5 us
  transfers between devices with their start and end apart: 1, of which 1 were waited for; matrix products, arithmetic and copies ran while one was open for 0% of the time, Pallas kernels for 0%

profile of v1, /device:TPU:0, one launch (start us, length us, event | category | flops | bytes accessed | tf_op | source)
XLA Modules:
  0.0 118.3 jit_solution(12325252317265854054)
XLA Ops:
  7.2 0.0 all-gather.3.cloned.1.call-start
  7.2 0.7 all-gather.3.cloned.1.call-update
  7.9 24.1 %all-gather = bf16[16,96,64]{1,2,0:T(8,128)(2,1)S(1)} all-gather(bf16[1,96,64]{1,2,0:T(8,128)(2,1)} %bitcast.7), channel_id=1, replica_groups=mesh['groups'=2,'col'=8,'row'=2] {'col','row'}, dimensions={0}, use_global_device_ids=true | all-gather | bytes 208896 | tf_op jit(solution)/shard_map/all_gather | solution.py:120
  31.9 0.2 copy.5
  32.1 0.3 reshape.5
  32.4 20.5 %all-gather.3.cloned.1.call-done.sketch = f32[1536,256]{1,0:T(8,128)} async-done(((f32[96,256]{1,0:T(8,128)}), f32[1536,256]{1,0:T(8,128)}) %all-gather.3.cloned.1.call-update) | async-done | bytes 1572880 | tf_op jit(solution)/shard_map/all_gather | solution.py:121
  52.8 0.0 copy-start
  52.8 1.4 %copy-done = f32[1536,256]{1,0:T(8,128)S(1)} copy-done((f32[1536,256]{1,0:T(8,128)S(1)}, f32[1536,256]{1,0:T(8,128)}, u32[]{:S(2)}) %copy-start) | copy-done | bytes 1572888
  54.3 57.2 %shard_map.41 = (f32[96,256]{1,0:T(8,128)}, f32[256,256]{1,0:T(8,128)}) custom-call(bf16[64,1536]{1,0:T(8,128)(2,1)S(1)} %bitcast.6, f32[1536,256]{1,0:T(8,128)S(1)} %copy-done), custom_call_target="tpu_custom_call" | custom-call | tf_op jit(solution)/shard_map/pallas_call | solution.py:122
Async XLA Ops:
  7.2 45.7 %all-gather.3.cloned.1.call-start = ((), (), s32[]{:S(2)}) async-start(), calls=%async_computation | async-start | bytes 1671168 | tf_op jit(solution)/shard_map/all_gather | solution.py:121
  52.8 1.4 %copy-start = (f32[1536,256]{1,0:T(8,128)S(1)}, f32[1536,256]{1,0:T(8,128)}, u32[]{:S(2)}) copy-start(f32[1536,256]{1,0:T(8,128)} %all-gather.3.cloned.1.call-done.sketch) | copy-start | bytes 4718596
Sparse Core Ops, SparseCore 0:
  10.3 42.5 all-gather.2

commit v2 on v1

--- a/solution.py
+++ b/solution.py
@@ -12,6 +12,7 @@
 MAX_POINTS = 2048
 ROWS = 256
 HALF = 128
+MESH = pl.DeviceIdType.MESH
 
 
 def dot(a, b, dims, precision=None):
@@ -60,18 +61,80 @@
     return upper, jnp.concatenate(done_i, axis=0)
 
 
+def gather_kernel(own_pts, own_sketch, pts, sketch, *sems):
+    own = own_sketch.shape[0]
+    group = lax.axis_index("groups")
+    col, core = lax.axis_index("col"), lax.axis_index("row")
+    depth = lax.axis_size("col") // 2
+    z, y = col // 2, lax.rem(col, 2)
+
+    def device(z_of, y_of, core_of):
+        return (group, z_of * 2 + y_of, core_of)
+
+    def rows(z_of, y_of, core_of):
+        slot = (core_of * 2 + y_of) * depth + z_of
+        return pl.ds(pl.multiple_of(slot * own, 16), own)
+
+    along_z = [device(lax.rem(z + d, depth), y, core) for d in range(1, depth)]
+    y_peer, core_peer = device(z, 1 - y, core), device(z, y, 1 - core)
+    barrier = pltpu.get_barrier_semaphore()
+    for peer in along_z + [y_peer, core_peer]:
+        pl.semaphore_signal(barrier, inc=1, device_id=peer, device_id_type=MESH)
+    mine = rows(z, y, core)
+    pts[mine, :] = own_pts[...]
+    sketch[mine, :] = own_sketch[...]
+    pl.semaphore_wait(barrier, depth + 1)
+
+    def send(full, at, peer, number, send_sem, recv_sem):
+        copy = pltpu.make_async_remote_copy(
+            src_ref=full.at[at, :],
+            dst_ref=full.at[at, :],
+            send_sem=send_sem.at[number],
+            recv_sem=recv_sem.at[number],
+            device_id=peer,
+            device_id_type=MESH,
+        )
+        copy.start()
+        return copy
+
+    arrays = [(pts, sems[0], sems[1]), (sketch, sems[2], sems[3])]
+    z_copies, y_copies, c_copies = [[], []], [[], []], [[], []]
+    y_base, c_base = depth - 1, 2 * depth - 1
+    for n, (full, ss, rs) in enumerate(arrays):
+        for d in range(1, depth):
+            z_copies[n].append(send(full, mine, along_z[d - 1], d - 1, ss, rs))
+        y_copies[n].append(send(full, mine, y_peer, y_base, ss, rs))
+        c_copies[n].append(send(full, mine, core_peer, c_base, ss, rs))
+    for n, (full, ss, rs) in enumerate(arrays):
+        for d in range(1, depth):
+            at = rows(lax.rem(z - d + depth, depth), y, core)
+            z_copies[n][d - 1].wait_recv()
+            y_copies[n].append(send(full, at, y_peer, y_base + d, ss, rs))
+            c_copies[n].append(send(full, at, core_peer, c_base + d, ss, rs))
+        for d in range(depth):
+            at = rows(lax.rem(z - d + depth, depth), 1 - y, core)
+            y_copies[n][d].wait_recv()
+            c_copies[n].append(send(full, at, core_peer, c_base + depth + d, ss, rs))
+    for n in range(2):
+        for copy in c_copies[n]:
+            copy.wait_recv()
+        for copy in z_copies[n] + y_copies[n] + c_copies[n]:
+            copy.wait_send()
+
+
 def part_kernel(gamma, pts, sketch, basis, factor, high, low, v, vh, vl, y, inv):
-    feats, count = pts.shape
+    count, feats = pts.shape
     own = basis.shape[0]
-    me = lax.axis_index("col") * lax.axis_size("row") + lax.axis_index("row")
+    col, core = lax.axis_index("col"), lax.axis_index("row")
+    me = (core * 2 + lax.rem(col, 2)) * (lax.axis_size("col") // 2) + col // 2
     all_f = pts[...].astype(jnp.float32)
-    all_sq = jnp.sum(all_f * all_f, axis=0, keepdims=True)
-    ones = jnp.ones((feats, HALF), jnp.float32)
+    ones = jnp.ones((8, feats), jnp.float32)
+    all_sq = dot(ones, all_f * all_f, ((1,), (1,)), HIGHEST)[:1]
     for at in range(0, count, ROWS):
-        rows = pts[:, at : at + ROWS]
+        rows = pts[at : at + ROWS, :]
         rows_f = rows.astype(jnp.float32)
-        rows_sq = dot(rows_f * rows_f, ones, ((0,), (0,)), HIGHEST)[:, :1]
-        cross = dot(rows, pts[...], ((0,), (0,)))
+        rows_sq = jnp.sum(rows_f * rows_f, axis=1, keepdims=True)
+        cross = dot(rows, pts[...], ((1,), (1,)))
         h, l = split(jnp.exp(-gamma * (rows_sq + all_sq - 2.0 * cross)))
         high[at : at + ROWS] = h
         low[at : at + ROWS] = l
@@ -117,8 +180,20 @@
     rank = sketch.shape[1]
     count = own * lax.axis_size("col") * lax.axis_size("row")
     gamma = ((count / 32.0) ** (2.0 / feats) - 1.0) / 4.0
-    pts = lax.all_gather(points, ("col", "row"), axis=1, tiled=True)
-    full = lax.all_gather(sketch, ("col", "row"), axis=0, tiled=True)
+    copies = 2 * (lax.axis_size("col") // 2) * 2 - 1
+    pts, full = pl.pallas_call(
+        gather_kernel,
+        out_shape=(
+            jax.ShapeDtypeStruct((count, feats), points.dtype),
+            jax.ShapeDtypeStruct((count, rank), sketch.dtype),
+        ),
+        in_specs=[pl.BlockSpec(memory_space=pltpu.VMEM)] * 2,
+        out_specs=[pl.BlockSpec(memory_space=pltpu.VMEM)] * 2,
+        scratch_shapes=[pltpu.SemaphoreType.DMA((copies,))] * 4,
+        compiler_params=pltpu.CompilerParams(
+            collective_id=0, has_side_effects=True, vmem_limit_bytes=8 * 1024 * 1024
+        ),
+    )(points.T, sketch)
     return pl.pallas_call(
         functools.partial(part_kernel, gamma),
         out_shape=(
@@ -190,7 +265,8 @@
 def local(points, sketch):
     count = points.shape[1] * lax.axis_size("col") * lax.axis_size("row")
     small = count <= MAX_POINTS and count % ROWS == 0
-    if small and sketch.shape[1] == 2 * HALF and points.shape[1] % 8 == 0:
+    pairs = lax.axis_size("col") % 2 == 0 and lax.axis_size("row") == 2
+    if small and pairs and sketch.shape[1] == 2 * HALF and points.shape[1] % 16 == 0:
         return whole_part(points, sketch)
     return split_part(points, sketch)
 

time: 118 us -> 83.1 us (0.70)
  blocking collectives: 24.1 us -> 0 us
  Pallas kernels: 57.2 us -> 80.5 us
  waiting for transfers between devices: 21.1 us -> 0 us
  between operations: 14 us -> 0.65 us
    all_gather x1 -> x0, blocking collectives: 24.1 us -> none  [whole_part(): pts = lax.all_gather(points, ('col', 'row'), axis=1, tiled=True)]
    pallas_call x0 -> x1, Pallas kernels: none -> 23.1 us  [whole_part(): pl.pallas_call(gather_kernel, out_shape=(jax.ShapeDtypeStruct((count, fea...]
    all_gather x1 -> x0, waiting for transfers between devices: 20.5 us -> none  [whole_part(): full = lax.all_gather(sketch, ('col', 'row'), axis=0, tiled=True)]
  transfers between devices with their start and end apart: 1 -> 0, of which waited for: 1 -> 0; matrix products, arithmetic and copies ran while one was open for 0% -> 0% of each run, Pallas kernels for 0% -> 0%
where the time goes in v2:
time: 83.1 us; the launch traced here: 82.9 us
  Pallas kernels  80.5 us (97%)
  local copies, waits for them, and re-layouts  1.71 us (2%)
    pallas_call x1, Pallas kernels, whole_part(): pl.pallas_call(functools.partial(part_kernel, gamma), out_shape=(jax.Shap...  57.4 us
    pallas_call x1, Pallas kernels, whole_part(): pl.pallas_call(gather_kernel, out_shape=(jax.ShapeDtypeStruct((count, fea...  23.1 us
    unnamed x3, local copies, waits for them, and re-layouts  1.71 us

profile of v2, /device:TPU:0, one launch (start us, length us, event | category | flops | bytes accessed | tf_op | source)
XLA Modules:
  0.0 82.9 jit_solution(1490323065894799036)
XLA Ops:
  0.6 0.8 copy.4
  1.4 0.0 copy-start
  1.5 0.9 %copy-done = f32[96,256]{1,0:T(8,128)S(1)} copy-done((f32[96,256]{1,0:T(8,128)S(1)}, f32[96,256]{1,0:T(8,128)}, u32[]{:S(2)}) %copy-start) | copy-done | bytes 98328
  2.3 23.1 %shard_map.41 = (bf16[1536,64]{1,0:T(8,128)(2,1)S(1)}, f32[1536,256]{1,0:T(8,128)S(1)}) custom-call(bf16[96,64]{1,0:T(8,128)(2,1)S(1)} %bitcast.1, f32[96,256]{1,0:T(8,128)S(1)} %copy-done), custom_call_target="tpu_custom_call" | custom-call | tf_op jit(solution)/shard_map/pallas_call | solution.py:184
  25.5 57.4 %shard_map.42 = (f32[96,256]{1,0:T(8,128)}, f32[256,256]{1,0:T(8,128)}) custom-call(bf16[1536,64]{1,0:T(8,128)(2,1)S(1)} %get-tuple-element.4.pts, f32[1536,256]{1,0:T(8,128)S(1)} %get-tuple-element.5.sketch), custom_call_target="tpu_custom_call" | custom-call | tf_op jit(solution)/shard_map/pallas_call | solution.py:197
Async XLA Ops:
  1.4 0.9 %copy-start = (f32[96,256]{1,0:T(8,128)S(1)}, f32[96,256]{1,0:T(8,128)}, u32[]{:S(2)}) copy-start(f32[96,256]{1,0:T(8,128)} %own_sketch.1) | copy-start | bytes 294916

commit v3 on v2

--- a/solution.py
+++ b/solution.py
@@ -61,7 +61,8 @@
     return upper, jnp.concatenate(done_i, axis=0)
 
 
-def gather_kernel(own_pts, own_sketch, pts, sketch, *sems):
+def gather_kernel(gamma, own_pts, own_sketch, high, low, sketch, pts, *sems):
+    count, feats = pts.shape
     own = own_sketch.shape[0]
     group = lax.axis_index("groups")
     col, core = lax.axis_index("col"), lax.axis_index("row")
@@ -100,44 +101,70 @@
     arrays = [(pts, sems[0], sems[1]), (sketch, sems[2], sems[3])]
     z_copies, y_copies, c_copies = [[], []], [[], []], [[], []]
     y_base, c_base = depth - 1, 2 * depth - 1
-    for n, (full, ss, rs) in enumerate(arrays):
+
+    def first(n):
+        full, ss, rs = arrays[n]
         for d in range(1, depth):
             z_copies[n].append(send(full, mine, along_z[d - 1], d - 1, ss, rs))
         y_copies[n].append(send(full, mine, y_peer, y_base, ss, rs))
         c_copies[n].append(send(full, mine, core_peer, c_base, ss, rs))
-    for n, (full, ss, rs) in enumerate(arrays):
-        for d in range(1, depth):
-            at = rows(lax.rem(z - d + depth, depth), y, core)
-            z_copies[n][d - 1].wait_recv()
-            y_copies[n].append(send(full, at, y_peer, y_base + d, ss, rs))
-            c_copies[n].append(send(full, at, core_peer, c_base + d, ss, rs))
-        for d in range(depth):
-            at = rows(lax.rem(z - d + depth, depth), 1 - y, core)
-            y_copies[n][d].wait_recv()
-            c_copies[n].append(send(full, at, core_peer, c_base + depth + d, ss, rs))
+
+    def after_z(n, d):
+        full, ss, rs = arrays[n]
+        at = rows(lax.rem(z - d + depth, depth), y, core)
+        z_copies[n][d - 1].wait_recv()
+        y_copies[n].append(send(full, at, y_peer, y_base + d, ss, rs))
+        c_copies[n].append(send(full, at, core_peer, c_base + d, ss, rs))
+
+    def after_y(n, d):
+        full, ss, rs = arrays[n]
+        at = rows(lax.rem(z - d + depth, depth), 1 - y, core)
+        y_copies[n][d].wait_recv()
+        c_copies[n].append(send(full, at, core_peer, c_base + depth + d, ss, rs))
+
+    first(0)
+    for d in range(1, depth):
+        after_z(0, d)
+    first(1)
+    for d in range(depth):
+        after_y(0, d)
+    for copy in c_copies[0]:
+        copy.wait_recv()
+
+    hops = [functools.partial(after_z, 1, d) for d in range(1, depth)]
+    hops += [functools.partial(after_y, 1, d) for d in range(depth)]
+    blocks = count // ROWS
+    gaps = max(blocks - 1, 1)
+    all_f = pts[...].astype(jnp.float32)
+    ones = jnp.ones((8, feats), jnp.float32)
+    all_sq = dot(ones, all_f * all_f, ((1,), (1,)), HIGHEST)[:1]
+    for b in range(blocks):
+        at = b * ROWS
+        block = pts[at : at + ROWS, :]
+        block_f = block.astype(jnp.float32)
+        block_sq = jnp.sum(block_f * block_f, axis=1, keepdims=True)
+        cross = dot(block, pts[...], ((1,), (1,)))
+        h, l = split(jnp.exp(-gamma * (block_sq + all_sq - 2.0 * cross)))
+        high[at : at + ROWS] = h
+        low[at : at + ROWS] = l
+        if b > 0:
+            for hop in hops[(b - 1) * len(hops) // gaps : b * len(hops) // gaps]:
+                hop()
+    if blocks == 1:
+        for hop in hops:
+            hop()
+    for copy in c_copies[1]:
+        copy.wait_recv()
     for n in range(2):
-        for copy in c_copies[n]:
-            copy.wait_recv()
         for copy in z_copies[n] + y_copies[n] + c_copies[n]:
             copy.wait_send()
 
 
-def part_kernel(gamma, pts, sketch, basis, factor, high, low, v, vh, vl, y, inv):
-    count, feats = pts.shape
+def part_kernel(high, low, sketch, basis, factor, v, vh, vl, y, inv):
+    count = high.shape[0]
     own = basis.shape[0]
     col, core = lax.axis_index("col"), lax.axis_index("row")
     me = (core * 2 + lax.rem(col, 2)) * (lax.axis_size("col") // 2) + col // 2
-    all_f = pts[...].astype(jnp.float32)
-    ones = jnp.ones((8, feats), jnp.float32)
-    all_sq = dot(ones, all_f * all_f, ((1,), (1,)), HIGHEST)[:1]
-    for at in range(0, count, ROWS):
-        rows = pts[at : at + ROWS, :]
-        rows_f = rows.astype(jnp.float32)
-        rows_sq = jnp.sum(rows_f * rows_f, axis=1, keepdims=True)
-        cross = dot(rows, pts[...], ((1,), (1,)))
-        h, l = split(jnp.exp(-gamma * (rows_sq + all_sq - 2.0 * cross)))
-        high[at : at + ROWS] = h
-        low[at : at + ROWS] = l
     v[...] = sketch[...]
 
     def one_pass(step, carry):
@@ -181,38 +208,38 @@
     count = own * lax.axis_size("col") * lax.axis_size("row")
     gamma = ((count / 32.0) ** (2.0 / feats) - 1.0) / 4.0
     copies = 2 * (lax.axis_size("col") // 2) * 2 - 1
-    pts, full = pl.pallas_call(
-        gather_kernel,
+    high, low, full = pl.pallas_call(
+        functools.partial(gather_kernel, gamma),
         out_shape=(
-            jax.ShapeDtypeStruct((count, feats), points.dtype),
+            jax.ShapeDtypeStruct((count, count), jnp.bfloat16),
+            jax.ShapeDtypeStruct((count, count), jnp.bfloat16),
             jax.ShapeDtypeStruct((count, rank), sketch.dtype),
         ),
         in_specs=[pl.BlockSpec(memory_space=pltpu.VMEM)] * 2,
-        out_specs=[pl.BlockSpec(memory_space=pltpu.VMEM)] * 2,
-        scratch_shapes=[pltpu.SemaphoreType.DMA((copies,))] * 4,
+        out_specs=[pl.BlockSpec(memory_space=pltpu.VMEM)] * 3,
+        scratch_shapes=[pltpu.VMEM((count, feats), points.dtype)]
+        + [pltpu.SemaphoreType.DMA((copies,))] * 4,
         compiler_params=pltpu.CompilerParams(
-            collective_id=0, has_side_effects=True, vmem_limit_bytes=8 * 1024 * 1024
+            collective_id=0, has_side_effects=True, vmem_limit_bytes=24 * 1024 * 1024
         ),
     )(points.T, sketch)
     return pl.pallas_call(
-        functools.partial(part_kernel, gamma),
+        part_kernel,
         out_shape=(
             jax.ShapeDtypeStruct((own, rank), jnp.float32),
             jax.ShapeDtypeStruct((rank, rank), jnp.float32),
         ),
-        in_specs=[pl.BlockSpec(memory_space=pltpu.VMEM)] * 2,
+        in_specs=[pl.BlockSpec(memory_space=pltpu.VMEM)] * 3,
         out_specs=[pl.BlockSpec(memory_space=pltpu.VMEM)] * 2,
         scratch_shapes=[
-            pltpu.VMEM((count, count), jnp.bfloat16),
-            pltpu.VMEM((count, count), jnp.bfloat16),
             pltpu.VMEM((count, rank), jnp.float32),
             pltpu.VMEM((count, rank), jnp.bfloat16),
             pltpu.VMEM((count, rank), jnp.bfloat16),
             pltpu.VMEM((count, rank), jnp.float32),
             pltpu.VMEM((rank, rank), jnp.float32),
         ],
-        compiler_params=pltpu.CompilerParams(vmem_limit_bytes=50 * 1024 * 1024),
-    )(pts, full)
+        compiler_params=pltpu.CompilerParams(vmem_limit_bytes=28 * 1024 * 1024),
+    )(high, low, full)
 
 
 def kernel_rows(block_t, cols_t, gamma):

time: 83.1 us -> 80.4 us (0.968)
  Pallas kernels: 80.5 us -> 77.8 us
    pallas_call x2, Pallas kernels: 80.5 us -> 77.8 us  [the longest x1 53.3 us: whole_part(): pl.pallas_call(part_kernel, out_shape=(jax.ShapeDtypeStruct((own, rank),...]
where the time goes in v3:
time: 80.4 us; the launch traced here: 80.2 us
  Pallas kernels  77.8 us (97%)
  local copies, waits for them, and re-layouts  1.71 us (2%)
    pallas_call x1, Pallas kernels, whole_part(): pl.pallas_call(part_kernel, out_shape=(jax.ShapeDtypeStruct((own, rank),...  53.3 us
    pallas_call x1, Pallas kernels, whole_part(): pl.pallas_call(functools.partial(gather_kernel, gamma), out_shape=(jax.Sh...  24.5 us
    unnamed x3, local copies, waits for them, and re-layouts  1.71 us

profile of v3, /device:TPU:0, one launch (start us, length us, event | category | flops | bytes accessed | tf_op | source)
XLA Modules:
  0.0 80.2 jit_solution(3345624162216739229)
XLA Ops:
  0.6 0.8 %copy.4 = bf16[64,96]{0,1:T(8,128)(2,1)S(1)} copy(bf16[64,96]{1,0:T(8,128)(2,1)} %param.2) | data formatting | bytes 24576 | tf_op args[0]
  1.4 0.0 copy-start
  1.5 0.9 %copy-done = f32[96,256]{1,0:T(8,128)S(1)} copy-done((f32[96,256]{1,0:T(8,128)S(1)}, f32[96,256]{1,0:T(8,128)}, u32[]{:S(2)}) %copy-start) | copy-done | bytes 98328
  2.3 24.5 %shard_map.41 = (bf16[1536,1536]{1,0:T(8,128)(2,1)S(1)}, bf16[1536,1536]{1,0:T(8,128)(2,1)S(1)}, f32[1536,256]{1,0:T(8,128)S(1)}) custom-call(bf16[96,64]{1,0:T(8,128)(2,1)S(1)} %bitcast.1, f32[96,256]{1,0:T(8,128)S(1)} %copy-done), custom_call_target="tpu_custom_call" | custom-call | tf_op jit(solution)/shard_map/pallas_call | solution.py:211
  26.8 53.3 %shard_map.42 = (f32[96,256]{1,0:T(8,128)}, f32[256,256]{1,0:T(8,128)}) custom-call(bf16[1536,1536]{1,0:T(8,128)(2,1)S(1)} %get-tuple-element.5.high, bf16[1536,1536]{1,0:T(8,128)(2,1)S(1)} %get-tuple-element.6.low, f32[1536,256]{1,0:T(8,128)S(1)} %get-tuple-element.7.sketch), custom_call_target="tpu_custom_call" | custom-call | tf_op jit(solution)/shard_map/pallas_call | solution.py:226
Async XLA Ops:
  1.4 0.9 %copy-start = (f32[96,256]{1,0:T(8,128)S(1)}, f32[96,256]{1,0:T(8,128)}, u32[]{:S(2)}) copy-start(f32[96,256]{1,0:T(8,128)} %own_sketch.1) | copy-start | bytes 294916

commit v4 on v3

--- a/solution.py
+++ b/solution.py
@@ -123,9 +123,9 @@
         c_copies[n].append(send(full, at, core_peer, c_base + depth + d, ss, rs))
 
     first(0)
+    first(1)
     for d in range(1, depth):
         after_z(0, d)
-    first(1)
     for d in range(depth):
         after_y(0, d)
     for copy in c_copies[0]:
@@ -181,7 +181,13 @@
 
         lax.fori_loop(0, count // ROWS, apply_rows, 0)
         ym = y[...]
-        gram = dot(ym, ym, ((0,), (0,)), HIGHEST) / count
+        h, l = split(ym)
+        vh[...] = h
+        vl[...] = l
+        d = ((0,), (0,))
+        cross = dot(vh[...], vl[...], d)
+        gram = dot(vh[...], vh[...], d) + (cross + cross.T + dot(vl[...], vl[...], d))
+        gram = gram / count
         u11, i11 = factor_block(gram[:HALF, :HALF])
         u12 = dot(i11, gram[:HALF, HALF:], ((1,), (0,)), HIGHEST)
         rest = gram[HALF:, HALF:] - dot(u12, u12, ((0,), (0,)), HIGHEST)
@@ -195,11 +201,16 @@
         inv[:HALF, HALF:] = jnp.zeros_like(i11)
         inv[HALF:, :HALF] = i21
         inv[HALF:, HALF:] = i22
-        v[...] = dot(ym, inv[...], ((1,), (1,)), HIGHEST)
+
+        @pl.when(step < PASSES)
+        def _():
+            v[...] = dot(y[...], inv[...], ((1,), (1,)), HIGHEST)
+
         return carry
 
     lax.fori_loop(0, PASSES + 1, one_pass, 0)
-    basis[...] = v[pl.ds(pl.multiple_of(me * own, 8), own), :]
+    mine = y[pl.ds(pl.multiple_of(me * own, 8), own), :]
+    basis[...] = dot(mine, inv[...], ((1,), (1,)), HIGHEST)
 
 
 def whole_part(points, sketch):

time: 80.4 us -> 75.9 us (0.944)
  Pallas kernels: 77.8 us -> 73.3 us
    pallas_call x1, Pallas kernels: 53.3 us -> 46.4 us  [whole_part(): pl.pallas_call(part_kernel, out_shape=(jax.ShapeDtypeStruct((own, rank),...]
    pallas_call x1, Pallas kernels: 24.5 us -> 26.9 us  [whole_part(): pl.pallas_call(functools.partial(gather_kernel, gamma), out_shape=(jax.Sh...]
where the time goes in v4:
time: 75.9 us; the launch traced here: 75.7 us
  Pallas kernels  73.3 us (97%)
  local copies, waits for them, and re-layouts  1.71 us (2%)
    pallas_call x1, Pallas kernels, whole_part(): pl.pallas_call(part_kernel, out_shape=(jax.ShapeDtypeStruct((own, rank),...  46.4 us
    pallas_call x1, Pallas kernels, whole_part(): pl.pallas_call(functools.partial(gather_kernel, gamma), out_shape=(jax.Sh...  26.9 us
    unnamed x3, local copies, waits for them, and re-layouts  1.71 us

profile of v4, /device:TPU:0, one launch (start us, length us, event | category | flops | bytes accessed | tf_op | source)
XLA Modules:
  0.0 75.7 jit_solution(15442043382882160643)
XLA Ops:
  0.6 0.8 %copy.4 = bf16[64,96]{0,1:T(8,128)(2,1)S(1)} copy(bf16[64,96]{1,0:T(8,128)(2,1)} %param.2) | data formatting | bytes 24576 | tf_op args[0]
  1.4 0.0 copy-start
  1.5 0.9 %copy-done = f32[96,256]{1,0:T(8,128)S(1)} copy-done((f32[96,256]{1,0:T(8,128)S(1)}, f32[96,256]{1,0:T(8,128)}, u32[]{:S(2)}) %copy-start) | copy-done | bytes 98328
  2.3 26.9 %shard_map.41 = (bf16[1536,1536]{1,0:T(8,128)(2,1)S(1)}, bf16[1536,1536]{1,0:T(8,128)(2,1)S(1)}, f32[1536,256]{1,0:T(8,128)S(1)}) custom-call(bf16[96,64]{1,0:T(8,128)(2,1)S(1)} %bitcast.1, f32[96,256]{1,0:T(8,128)S(1)} %copy-done), custom_call_target="tpu_custom_call" | custom-call | tf_op jit(solution)/shard_map/pallas_call | solution.py:222
  29.3 46.4 %shard_map.42 = (f32[96,256]{1,0:T(8,128)}, f32[256,256]{1,0:T(8,128)}) custom-call(bf16[1536,1536]{1,0:T(8,128)(2,1)S(1)} %get-tuple-element.5.high, bf16[1536,1536]{1,0:T(8,128)(2,1)S(1)} %get-tuple-element.6.low, f32[1536,256]{1,0:T(8,128)S(1)} %get-tuple-element.7.sketch), custom_call_target="tpu_custom_call" | custom-call | tf_op jit(solution)/shard_map/pallas_call | solution.py:237
Async XLA Ops:
  1.4 0.9 %copy-start = (f32[96,256]{1,0:T(8,128)S(1)}, f32[96,256]{1,0:T(8,128)}, u32[]{:S(2)}) copy-start(f32[96,256]{1,0:T(8,128)} %own_sketch.1) | copy-start | bytes 294916

commit v5 on v4

--- a/solution.py
+++ b/solution.py
@@ -123,9 +123,9 @@
         c_copies[n].append(send(full, at, core_peer, c_base + depth + d, ss, rs))
 
     first(0)
-    first(1)
     for d in range(1, depth):
         after_z(0, d)
+    first(1)
     for d in range(depth):
         after_y(0, d)
     for copy in c_copies[0]:
@@ -160,18 +160,16 @@
             copy.wait_send()
 
 
-def part_kernel(high, low, sketch, basis, factor, v, vh, vl, y, inv):
+def part_kernel(high, low, sketch, basis, factor, vh, vl, y, inv):
     count = high.shape[0]
     own = basis.shape[0]
     col, core = lax.axis_index("col"), lax.axis_index("row")
     me = (core * 2 + lax.rem(col, 2)) * (lax.axis_size("col") // 2) + col // 2
-    v[...] = sketch[...]
+    h, l = split(sketch[...])
+    vh[...] = h
+    vl[...] = l
 
     def one_pass(step, carry):
-        h, l = split(v[...])
-        vh[...] = h
-        vl[...] = l
-
         def apply_rows(b, c):
             at = pl.ds(pl.multiple_of(b * ROWS, ROWS), ROWS)
             kh, kl = high[at, :], low[at, :]
@@ -204,7 +202,9 @@
 
         @pl.when(step < PASSES)
         def _():
-            v[...] = dot(y[...], inv[...], ((1,), (1,)), HIGHEST)
+            h, l = split(dot(y[...], inv[...], ((1,), (1,)), HIGHEST))
+            vh[...] = h
+            vl[...] = l
 
         return carry
 
@@ -243,7 +243,6 @@
         in_specs=[pl.BlockSpec(memory_space=pltpu.VMEM)] * 3,
         out_specs=[pl.BlockSpec(memory_space=pltpu.VMEM)] * 2,
         scratch_shapes=[
-            pltpu.VMEM((count, rank), jnp.float32),
             pltpu.VMEM((count, rank), jnp.bfloat16),
             pltpu.VMEM((count, rank), jnp.bfloat16),
             pltpu.VMEM((count, rank), jnp.float32),

time: 75.9 us -> 72.9 us (0.960)
  Pallas kernels: 73.3 us -> 70.3 us
    pallas_call x1, Pallas kernels: 26.9 us -> 24.5 us  [whole_part(): pl.pallas_call(functools.partial(gather_kernel, gamma), out_shape=(jax.Sh...]
where the time goes in v5:
time: 72.9 us; the launch traced here: 72.7 us
  Pallas kernels  70.3 us (96%)
  local copies, waits for them, and re-layouts  1.71 us (2%)
    pallas_call x1, Pallas kernels, whole_part(): pl.pallas_call(part_kernel, out_shape=(jax.ShapeDtypeStruct((own, rank),...  45.9 us
    pallas_call x1, Pallas kernels, whole_part(): pl.pallas_call(functools.partial(gather_kernel, gamma), out_shape=(jax.Sh...  24.5 us
    unnamed x3, local copies, waits for them, and re-layouts  1.71 us

profile of v5, /device:TPU:0, one launch (start us, length us, event | category | flops | bytes accessed | tf_op | source)
XLA Modules:
  0.0 72.7 jit_solution(4008357940985270817)
XLA Ops:
  0.6 0.8 %copy.4 = bf16[64,96]{0,1:T(8,128)(2,1)S(1)} copy(bf16[64,96]{1,0:T(8,128)(2,1)} %param.2) | data formatting | bytes 24576 | tf_op args[0]
  1.4 0.0 copy-start
  1.5 0.9 %copy-done = f32[96,256]{1,0:T(8,128)S(1)} copy-done((f32[96,256]{1,0:T(8,128)S(1)}, f32[96,256]{1,0:T(8,128)}, u32[]{:S(2)}) %copy-start) | copy-done | bytes 98328
  2.3 24.5 %shard_map.41 = (bf16[1536,1536]{1,0:T(8,128)(2,1)S(1)}, bf16[1536,1536]{1,0:T(8,128)(2,1)S(1)}, f32[1536,256]{1,0:T(8,128)S(1)}) custom-call(bf16[96,64]{1,0:T(8,128)(2,1)S(1)} %bitcast.1, f32[96,256]{1,0:T(8,128)S(1)} %copy-done), custom_call_target="tpu_custom_call" | custom-call | tf_op jit(solution)/shard_map/pallas_call | solution.py:222
  26.8 45.9 %shard_map.42 = (f32[96,256]{1,0:T(8,128)}, f32[256,256]{1,0:T(8,128)}) custom-call(bf16[1536,1536]{1,0:T(8,128)(2,1)S(1)} %get-tuple-element.5.high, bf16[1536,1536]{1,0:T(8,128)(2,1)S(1)} %get-tuple-element.6.low, f32[1536,256]{1,0:T(8,128)S(1)} %get-tuple-element.7.sketch), custom_call_target="tpu_custom_call" | custom-call | tf_op jit(solution)/shard_map/pallas_call | solution.py:237
Async XLA Ops:
  1.4 0.9 %copy-start = (f32[96,256]{1,0:T(8,128)S(1)}, f32[96,256]{1,0:T(8,128)}, u32[]{:S(2)}) copy-start(f32[96,256]{1,0:T(8,128)} %own_sketch.1) | copy-start | bytes 294916

commit v6 on v5

--- a/solution.py
+++ b/solution.py
@@ -162,6 +162,7 @@
 
 def part_kernel(high, low, sketch, basis, factor, vh, vl, y, inv):
     count = high.shape[0]
+    size = 2 * ROWS if count % (2 * ROWS) == 0 else ROWS
     own = basis.shape[0]
     col, core = lax.axis_index("col"), lax.axis_index("row")
     me = (core * 2 + lax.rem(col, 2)) * (lax.axis_size("col") // 2) + col // 2
@@ -171,13 +172,13 @@
 
     def one_pass(step, carry):
         def apply_rows(b, c):
-            at = pl.ds(pl.multiple_of(b * ROWS, ROWS), ROWS)
+            at = pl.ds(pl.multiple_of(b * size, size), size)
             kh, kl = high[at, :], low[at, :]
             d = ((1,), (0,))
             y[at, :] = dot(kh, vh[...], d) + (dot(kh, vl[...], d) + dot(kl, vh[...], d))
             return c
 
-        lax.fori_loop(0, count // ROWS, apply_rows, 0)
+        lax.fori_loop(0, count // size, apply_rows, 0)
         ym = y[...]
         h, l = split(ym)
         vh[...] = h

time: 72.9 us -> 71.4 us (0.979)
  Pallas kernels: 70.3 us -> 68.8 us
    pallas_call x1, Pallas kernels: 45.9 us -> 44.4 us  [whole_part(): pl.pallas_call(part_kernel, out_shape=(jax.ShapeDtypeStruct((own, rank),...]
where the time goes in v6:
time: 71.4 us; the launch traced here: 71.2 us
  Pallas kernels  68.8 us (96%)
  local copies, waits for them, and re-layouts  1.71 us (2%)
    pallas_call x1, Pallas kernels, whole_part(): pl.pallas_call(part_kernel, out_shape=(jax.ShapeDtypeStruct((own, rank),...  44.4 us
    pallas_call x1, Pallas kernels, whole_part(): pl.pallas_call(functools.partial(gather_kernel, gamma), out_shape=(jax.Sh...  24.5 us
    unnamed x3, local copies, waits for them, and re-layouts  1.71 us

profile of v6, /device:TPU:0, one launch (start us, length us, event | category | flops | bytes accessed | tf_op | source)
XLA Modules:
  0.0 71.2 jit_solution(14855104152705827924)
XLA Ops:
  0.6 0.8 %copy.4 = bf16[64,96]{0,1:T(8,128)(2,1)S(1)} copy(bf16[64,96]{1,0:T(8,128)(2,1)} %param.2) | data formatting | bytes 24576 | tf_op args[0]
  1.4 0.0 copy-start
  1.5 0.9 %copy-done = f32[96,256]{1,0:T(8,128)S(1)} copy-done((f32[96,256]{1,0:T(8,128)S(1)}, f32[96,256]{1,0:T(8,128)}, u32[]{:S(2)}) %copy-start) | copy-done | bytes 98328
  2.3 24.5 %shard_map.41 = (bf16[1536,1536]{1,0:T(8,128)(2,1)S(1)}, bf16[1536,1536]{1,0:T(8,128)(2,1)S(1)}, f32[1536,256]{1,0:T(8,128)S(1)}) custom-call(bf16[96,64]{1,0:T(8,128)(2,1)S(1)} %bitcast.1, f32[96,256]{1,0:T(8,128)S(1)} %copy-done), custom_call_target="tpu_custom_call" | custom-call | tf_op jit(solution)/shard_map/pallas_call | solution.py:223
  26.8 44.4 %shard_map.42 = (f32[96,256]{1,0:T(8,128)}, f32[256,256]{1,0:T(8,128)}) custom-call(bf16[1536,1536]{1,0:T(8,128)(2,1)S(1)} %get-tuple-element.5.high, bf16[1536,1536]{1,0:T(8,128)(2,1)S(1)} %get-tuple-element.6.low, f32[1536,256]{1,0:T(8,128)S(1)} %get-tuple-element.7.sketch), custom_call_target="tpu_custom_call" | custom-call | tf_op jit(solution)/shard_map/pallas_call | solution.py:238
Async XLA Ops:
  1.4 0.9 %copy-start = (f32[96,256]{1,0:T(8,128)S(1)}, f32[96,256]{1,0:T(8,128)}, u32[]{:S(2)}) copy-start(f32[96,256]{1,0:T(8,128)} %own_sketch.1) | copy-start | bytes 294916
